TPU v7x, 32 devices: a whole 2x2x4 slice. The times are simulated.
32 devices in a mesh: section: 4 (over x, core), expert: 2 (over y), dp: 4 (over z).
Axes of the slice: x: 2, y: 2, z: 4, core: 2. Of those that a mesh axis runs over, the one named last changes fastest.
Arguments:
- in_flight: bfloat16 [4, 2, 128, 3584], P('section', None, 'expert', 'dp'), may hold values from -6 to 6
- incoming: bfloat16 [2, 128, 3584], P(None, 'expert', 'dp'), may hold values from -6 to 6
- up_proj: bfloat16 [4, 32, 3584, 1152], P('section', 'expert', 'dp'), may hold values from -0.09375 to 0.09375
- down_proj: bfloat16 [4, 32, 1152, 3584], P('section', 'expert', None, 'dp'), may hold values from -0.1875 to 0.1875
- expert_ids: int32 [2, 4, 2, 128, 4], P(None, 'section', None, 'expert'), may hold values from 0 to 31, all different within a row; in each aligned block of 64 rows (0 to 63, 64 to 127, ..., all dimensions but the last counted through in order) at most 12 rows name the same one
- gate_logits: float32 [2, 4, 2, 128, 4], P(None, 'section', None, 'expert'), may hold values from -6 to 6
Outputs:
- states: bfloat16 [2, 4, 2, 128, 3584], P(None, 'section', None, 'expert', 'dp')
Inputs may be any that keep to these rules, and one draw needn't show every extreme that they name: `expert_ids`: each row names 4 different experts. In every aligned block of 64 rows, no expert is named by more than 12 rows, a bound that some block reaches.
All inputs are finite; a program needn't handle non-finite values.
Results may differ from a plain program's by a relative error of at most 0.015.
Values may be sent and summed in bfloat16 or wider, within the bound.
A program may use at most 192 MiB of HBM per device.

v0:
```python
import jax
import jax.numpy as jnp
from jax import lax
from jax.sharding import PartitionSpec as P

MB = 2
TICKS = 2
TOP = 4


def shifted(block, axis, distance):
    devices = range(lax.axis_size(axis))
    route = [(i - distance, i) for i in devices if i - distance in devices]
    return lax.ppermute(block, axis, route)


def gate_weights(logits):
    squashed = jax.nn.sigmoid(logits)
    return 2.5 * squashed / jnp.sum(squashed, axis=-1, keepdims=True)


def routing_slots(routing, experts, capacity):
    pair_ids = routing.reshape(-1)
    onehot = (pair_ids[:, None] == jnp.arange(experts, dtype=jnp.int32)[None, :]).astype(jnp.int32)
    before = jnp.cumsum(onehot, axis=0) - onehot
    slot_numbers = jnp.sum(before * onehot, axis=1)
    return pair_ids * capacity + slot_numbers


def experts_layer(tokens_in, routing, logits, up_weight, down_weight, capacity):
    batch_count, row_count, feature_width = tokens_in.shape
    per_device = up_weight.shape[0]
    groups = lax.axis_size("expert")
    experts = per_device * groups
    slots_total = experts * capacity
    slot_block = per_device * capacity
    flats = jnp.stack([routing_slots(routing[0], experts, capacity)])
    row_ids = jnp.broadcast_to(
        jnp.arange(row_count, dtype=jnp.int32)[:, None], (row_count, TOP)
    ).reshape(-1)

    def fill_table(slot_index):
        return jnp.full((slots_total,), -1, jnp.int32).at[slot_index].set(row_ids)

    sources = jax.vmap(fill_table)(flats)
    offset = jnp.arange(batch_count, dtype=jnp.int32)[:, None] * row_count
    source_index = jnp.where(sources >= 0, sources + offset, -1)
    source_index = (
        source_index.reshape(batch_count, groups, slot_block).transpose(1, 0, 2).reshape(-1)
    )
    flat_tokens = tokens_in.reshape(batch_count * row_count, feature_width)
    outgoing = jnp.where(
        (source_index >= 0)[:, None],
        flat_tokens[jnp.maximum(source_index, 0)],
        jnp.zeros((), flat_tokens.dtype),
    )
    outgoing = outgoing.reshape(groups, batch_count, per_device, capacity, feature_width)
    arrived = lax.all_to_all(outgoing, "expert", split_axis=0, concat_axis=0, tiled=True)
    partial_value = jnp.einsum(
        "gmxcd,xdf->gmxcf", arrived, up_weight, preferred_element_type=jnp.float32
    )
    rounded = lax.optimization_barrier(partial_value.astype(jnp.bfloat16)).astype(jnp.float32)
    summed = lax.psum(rounded.astype(jnp.bfloat16), "dp").astype(jnp.float32)
    hidden = jax.nn.silu(summed).astype(jnp.bfloat16)
    produced = jnp.einsum(
        "gmxcf,xfd->gmxcd", hidden, down_weight, preferred_element_type=jnp.float32
    ).astype(jnp.bfloat16)
    returned = lax.all_to_all(produced, "expert", split_axis=0, concat_axis=0, tiled=True)
    pick_index = (
        flats // slot_block * (batch_count * slot_block)
        + jnp.arange(batch_count, dtype=jnp.int32)[:, None] * slot_block
        + flats % slot_block
    )
    gathered = returned.reshape(-1, feature_width)[pick_index.reshape(-1)].reshape(
        batch_count, row_count, TOP, feature_width
    )
    weights = gate_weights(logits)
    routed_sum = jnp.einsum("mrk,mrkd->mrd", weights, gathered.astype(jnp.float32))
    return (tokens_in.astype(jnp.float32) + routed_sum).astype(jnp.bfloat16)


def body(in_flight, incoming, up_proj, down_proj, expert_ids, gate_logits):
    up_weight = up_proj[0]
    down_weight = down_proj[0]
    groups = lax.axis_size("expert")
    row_count = in_flight.shape[2]
    per_device = up_weight.shape[0]
    capacity = max(2, 3 * row_count * TOP // (2 * per_device * groups))
    current = in_flight[0]
    is_first = lax.axis_index("section") == 0
    states = []
    for tick_index in range(TICKS):
        if tick_index > 0:
            handed_on = shifted(states[-1], "section", 1)
            current = jnp.where(is_first, incoming, handed_on)
        routing = expert_ids[tick_index, 0]
        logits = gate_logits[tick_index, 0]
        pieces = [
            experts_layer(
                current[micro_index : micro_index + 1],
                routing[micro_index : micro_index + 1],
                logits[micro_index : micro_index + 1],
                up_weight,
                down_weight,
                capacity,
            )
            for micro_index in range(MB)
        ]
        result = jnp.concatenate(pieces, axis=0)
        states.append(result)
    return jnp.stack(states)[:, None]


def solution(mesh):
    return jax.shard_map(
        body,
        mesh=mesh,
        in_specs=(
            P("section", None, "expert", "dp"),
            P(None, "expert", "dp"),
            P("section", "expert", "dp", None),
            P("section", "expert", None, "dp"),
            P(None, "section", None, "expert", None),
            P(None, "section", None, "expert", None),
        ),
        out_specs=P(None, "section", None, "expert", "dp"),
        check_vma=False,
    )
```

profile of v0, /device:TPU:0, one launch (start us, length us, event | category | flops | bytes accessed | tf_op | source)
XLA Modules:
  0.0 419.1 jit_solution(6437509623442721821)
XLA Ops:
  8.9 1.4 scatter_custom_fusion
  11.3 2.3 gather_fusion
  15.1 4.2 %all-to-all-start = ((bf16[2,1,16,12,896]{4,2,3,1,0:T(8,128)(2,1)}), bf16[2,1,16,12,896]{4,2,3,1,0:T(8,128)(2,1)S(1)}, u32[]{:S(2)}, u32[]{:S(2)}) async-start(bf16[2,1,16,12,896]{4,2,3,1,0:T(8,128)(2,1)} %copy.45), calls=%async_computation | async-start | bytes 1376256 | tf_op jit(solution)/shard_map/all_to_all | solution.py:58
  20.8 1.4 scatter_custom_fusion.1
  22.2 2.3 gather_fusion.2
  28.3 1.5 all-to-all-done
  29.8 3.5 all-to-all-start.2
  33.9 14.3 %fusion.37 = bf16[2,1,16,12,1152]{4,3,0,2,1:T(8,128)(2,1)} fusion(bf16[1,16,896,1152]{3,2,1,0:T(8,128)(2,1)} %param.8, bf16[2,1,16,12,896]{4,2,3,1,0:T(8,128)(2,1)S(1)} %all-to-all-done), kind=kOutput, calls=%fused_computation.43 | convolution fusion | flops 793165824 | bytes 34603008 | tf_op jit(solution)/shard_map/gmxcd,xdf->gmxcf/dot_general | solution.py:59
  48.2 14.3 %fusion.34 = bf16[2,1,16,12,1152]{4,3,0,2,1:T(8,128)(2,1)} fusion(bf16[1,16,896,1152]{3,2,1,0:T(8,128)(2,1)} %param.8, bf16[2,1,16,12,896]{4,2,3,1,0:T(8,128)(2,1)S(1)} %all-to-all-done.2), kind=kOutput, calls=%fused_computation.42 | convolution fusion | flops 793165824 | bytes 34603008 | tf_op jit(solution)/shard_map/gmxcd,xdf->gmxcf/dot_general | solution.py:59
  63.5 97.1 %all-reduce.7.cloned.1.call-done = (bf16[2,1,16,12,1152]{4,3,0,2,1:T(8,128)(2,1)}, bf16[2,1,16,12,1152]{4,3,0,2,1:T(8,128)(2,1)}) async-done(((bf16[2,1,16,12,1152]{4,3,0,2,1:T(8,128)(2,1)}, bf16[2,1,16,12,1152]{4,3,0,2,1:T(8,128)(2,1)}), (bf16[2,1,16,12,1152]{4,3,0,2,1:T(8,128)(2,1)}, bf16[2,1,16,12,1152]{4,3,0,2,1:T(8,128)(2,1)})) %all-reduce.7.cloned.1.call-update) | async-done | bytes 1769488 | tf_op jit(solution)/shard_map/psum | solution.py:63
  160.6 15.8 %fusion.74 = bf16[2,1,16,12,896]{4,3,0,2,1:T(8,128)(2,1)S(1)} fusion(bf16[1,16,1152,896]{3,2,1,0:T(8,128)(2,1)} %param.9, bf16[2,1,16,12,1152]{4,3,0,2,1:T(8,128)(2,1)} %get-tuple-element.11), kind=kOutput, calls=%fused_computation.66 | convolution fusion | flops 795721728 | bytes 34603008 | tf_op jit(solution)/shard_map/gmxcf,xfd->gmxcd/dot_general | solution.py:65
  177.5 3.5 all-to-all-start.3
  181.0 12.5 %fusion.77 = bf16[2,1,16,12,896]{4,3,0,2,1:T(8,128)(2,1)S(1)} fusion(bf16[1,16,1152,896]{3,2,1,0:T(8,128)(2,1)} %param.9, bf16[2,1,16,12,1152]{4,3,0,2,1:T(8,128)(2,1)S(1)} %copy-done), kind=kOutput, calls=%fused_computation.67 | convolution fusion | flops 795721728 | bytes 34603008 | tf_op jit(solution)/shard_map/gmxcf,xfd->gmxcd/dot_general | solution.py:65
  194.6 3.5 all-to-all-start.1
  198.5 1.6 scatter_custom_fusion.2
  200.6 1.2 gather_fusion.3
  201.9 6.2 %all-to-all-done.1 = bf16[2,1,16,12,896]{4,2,3,1,0:T(8,128)(2,1)S(1)} async-done(((bf16[2,1,16,12,896]{4,2,3,1,0:T(8,128)(2,1)}), bf16[2,1,16,12,896]{4,2,3,1,0:T(8,128)(2,1)S(1)}, u32[]{:S(2)}, u32[]{:S(2)}) %all-to-all-start.1) | async-done | bytes 688160 | tf_op jit(solution)/shard_map/all_to_all | solution.py:68
  210.7 1.3 collective-permute-start
  212.0 1.4 scatter_custom_fusion.3
  213.7 2.3 gather_fusion.4
  217.3 3.5 all-to-all-start.4
  220.8 2.3 gather_fusion.6
  224.5 4.9 %all-to-all-done.4 = bf16[2,1,16,12,896]{4,2,3,1,0:T(8,128)(2,1)S(1)} async-done(((bf16[2,1,16,12,896]{4,2,3,1,0:T(8,128)(2,1)}), bf16[2,1,16,12,896]{4,2,3,1,0:T(8,128)(2,1)S(1)}, u32[]{:S(2)}, u32[]{:S(2)}) %all-to-all-start.4) | async-done | bytes 688160 | tf_op jit(solution)/shard_map/all_to_all | solution.py:58
  229.4 3.5 all-to-all-start.6
  233.2 14.3 %fusion.31 = bf16[2,1,16,12,1152]{4,3,0,2,1:T(8,128)(2,1)} fusion(bf16[1,16,896,1152]{3,2,1,0:T(8,128)(2,1)} %param.8, bf16[2,1,16,12,896]{4,2,3,1,0:T(8,128)(2,1)S(1)} %all-to-all-done.4), kind=kOutput, calls=%fused_computation.41 | convolution fusion | flops 793165824 | bytes 34603008 | tf_op jit(solution)/shard_map/gmxcd,xdf->gmxcf/dot_general | solution.py:59
  247.5 14.2 %fusion.28 = bf16[2,1,16,12,1152]{4,3,0,2,1:T(8,128)(2,1)} fusion(bf16[1,16,896,1152]{3,2,1,0:T(8,128)(2,1)} %param.8, bf16[2,1,16,12,896]{4,2,3,1,0:T(8,128)(2,1)S(1)} %all-to-all-done.6), kind=kOutput, calls=%fused_computation.40 | convolution fusion | flops 793165824 | bytes 34603008 | tf_op jit(solution)/shard_map/gmxcd,xdf->gmxcf/dot_general | solution.py:59
  261.8 99.0 %all-reduce.5.cloned.1.call-done = (bf16[2,1,16,12,1152]{4,3,0,2,1:T(8,128)(2,1)}, bf16[2,1,16,12,1152]{4,3,0,2,1:T(8,128)(2,1)}) async-done(((bf16[2,1,16,12,1152]{4,3,0,2,1:T(8,128)(2,1)}, bf16[2,1,16,12,1152]{4,3,0,2,1:T(8,128)(2,1)}), (bf16[2,1,16,12,1152]{4,3,0,2,1:T(8,128)(2,1)}, bf16[2,1,16,12,1152]{4,3,0,2,1:T(8,128)(2,1)})) %all-reduce.5.cloned.1.call-update) | async-done | bytes 1769488 | tf_op jit(solution)/shard_map/psum | solution.py:63
  360.8 15.8 %fusion.68 = bf16[2,1,16,12,896]{4,3,0,2,1:T(8,128)(2,1)S(1)} fusion(bf16[1,16,1152,896]{3,2,1,0:T(8,128)(2,1)} %param.9, bf16[2,1,16,12,1152]{4,3,0,2,1:T(8,128)(2,1)} %get-tuple-element.9), kind=kOutput, calls=%fused_computation.64 | convolution fusion | flops 795721728 | bytes 34603008 | tf_op jit(solution)/shard_map/gmxcf,xfd->gmxcd/dot_general | solution.py:65
  377.8 3.5 all-to-all-start.7
  381.3 12.5 %fusion.71 = bf16[2,1,16,12,896]{4,3,0,2,1:T(8,128)(2,1)S(1)} fusion(bf16[1,16,1152,896]{3,2,1,0:T(8,128)(2,1)} %param.9, bf16[2,1,16,12,1152]{4,3,0,2,1:T(8,128)(2,1)S(1)} %copy-done.1), kind=kOutput, calls=%fused_computation.65 | convolution fusion | flops 795721728 | bytes 34603008 | tf_op jit(solution)/shard_map/gmxcf,xfd->gmxcd/dot_general | solution.py:65
  394.9 3.8 all-to-all-start.5
  400.7 7.9 %all-to-all-done.5 = bf16[2,1,16,12,896]{4,2,3,1,0:T(8,128)(2,1)S(1)} async-done(((bf16[2,1,16,12,896]{4,2,3,1,0:T(8,128)(2,1)}), bf16[2,1,16,12,896]{4,2,3,1,0:T(8,128)(2,1)S(1)}, u32[]{:S(2)}, u32[]{:S(2)}) %all-to-all-start.5) | async-done | bytes 688160 | tf_op jit(solution)/shard_map/all_to_all | solution.py:68
  (158 shorter events, 27.8 us)
Async XLA Ops:
  15.1 14.7 %all-to-all-start = ((bf16[2,1,16,12,896]{4,2,3,1,0:T(8,128)(2,1)}), bf16[2,1,16,12,896]{4,2,3,1,0:T(8,128)(2,1)S(1)}, u32[]{:S(2)}, u32[]{:S(2)}) async-start(bf16[2,1,16,12,896]{4,2,3,1,0:T(8,128)(2,1)} %copy.45), calls=%async_computation | async-start | bytes 1376256 | tf_op jit(solution)/shard_map/all_to_all | solution.py:58
  27.5 20.7 %copy-start.5 = (s32[32,3]{0,1:T(4,128)}, s32[32,3]{0,1:T(4,128)S(1)}, u32[]{:S(2)}) copy-start(s32[32,3]{0,1:T(4,128)S(1)} %reduce-window.35) | copy-start | bytes 1156
  29.8 18.4 %all-to-all-start.2 = ((bf16[2,1,16,12,896]{4,2,3,1,0:T(8,128)(2,1)}), bf16[2,1,16,12,896]{4,2,3,1,0:T(8,128)(2,1)S(1)}, u32[]{:S(2)}, u32[]{:S(2)}) async-start(bf16[2,1,16,12,896]{4,2,3,1,0:T(8,128)(2,1)} %copy.54), calls=%async_computation.2 | async-start | bytes 1376256 | tf_op jit(solution)/shard_map/all_to_all | solution.py:58
  33.3 127.2 %all-reduce.7.cloned.1.call-start = ((), (), s32[]{:S(2)}) async-start(), calls=%async_computation.9 | async-start | bytes 4718592 | tf_op jit(solution)/shard_map/psum | solution.py:63
  62.5 0.7 slice-start
  62.5 0.8 copy-start.4
  176.4 4.6 %copy-start = (bf16[2,1,16,12,1152]{4,3,0,2,1:T(8,128)(2,1)S(1)}, bf16[2,1,16,12,1152]{4,3,0,2,1:T(8,128)(2,1)}, u32[]{:S(2)}) copy-start(bf16[2,1,16,12,1152]{4,3,0,2,1:T(8,128)(2,1)} %get-tuple-element.12) | copy-start | bytes 2654212
  177.5 17.1 %all-to-all-start.3 = ((bf16[2,1,16,12,896]{4,2,3,1,0:T(8,128)(2,1)}), bf16[2,1,16,12,896]{4,2,3,1,0:T(8,128)(2,1)S(1)}, u32[]{:S(2)}, u32[]{:S(2)}) async-start(bf16[2,1,16,12,896]{4,2,3,1,0:T(8,128)(2,1)} %copy.56), calls=%async_computation.3 | async-start | bytes 1376256 | tf_op jit(solution)/shard_map/all_to_all | solution.py:68
  194.6 13.5 %all-to-all-start.1 = ((bf16[2,1,16,12,896]{4,2,3,1,0:T(8,128)(2,1)}), bf16[2,1,16,12,896]{4,2,3,1,0:T(8,128)(2,1)S(1)}, u32[]{:S(2)}, u32[]{:S(2)}) async-start(bf16[2,1,16,12,896]{4,2,3,1,0:T(8,128)(2,1)} %copy.47), calls=%async_computation.1 | async-start | bytes 1376256 | tf_op jit(solution)/shard_map/all_to_all | solution.py:68
  209.6 1.0 copy-start.2
  209.6 4.0 copy-start.3
  210.7 2.9 collective-permute-start
  217.3 12.1 %all-to-all-start.4 = ((bf16[2,1,16,12,896]{4,2,3,1,0:T(8,128)(2,1)}), bf16[2,1,16,12,896]{4,2,3,1,0:T(8,128)(2,1)S(1)}, u32[]{:S(2)}, u32[]{:S(2)}) async-start(bf16[2,1,16,12,896]{4,2,3,1,0:T(8,128)(2,1)} %copy.63), calls=%async_computation.4 | async-start | bytes 1376256 | tf_op jit(solution)/shard_map/all_to_all | solution.py:58
  229.4 18.1 %all-to-all-start.6 = ((bf16[2,1,16,12,896]{4,2,3,1,0:T(8,128)(2,1)}), bf16[2,1,16,12,896]{4,2,3,1,0:T(8,128)(2,1)S(1)}, u32[]{:S(2)}, u32[]{:S(2)}) async-start(bf16[2,1,16,12,896]{4,2,3,1,0:T(8,128)(2,1)} %copy.72), calls=%async_computation.6 | async-start | bytes 1376256 | tf_op jit(solution)/shard_map/all_to_all | solution.py:58
  232.9 127.9 %all-reduce.5.cloned.1.call-start = ((), (), s32[]{:S(2)}) async-start(), calls=%async_computation.8 | async-start | bytes 4718592 | tf_op jit(solution)/shard_map/psum | solution.py:63
  376.6 4.6 %copy-start.1 = (bf16[2,1,16,12,1152]{4,3,0,2,1:T(8,128)(2,1)S(1)}, bf16[2,1,16,12,1152]{4,3,0,2,1:T(8,128)(2,1)}, u32[]{:S(2)}) copy-start(bf16[2,1,16,12,1152]{4,3,0,2,1:T(8,128)(2,1)} %get-tuple-element.10) | copy-start | bytes 2654212
  377.8 17.1 %all-to-all-start.7 = ((bf16[2,1,16,12,896]{4,2,3,1,0:T(8,128)(2,1)}), bf16[2,1,16,12,896]{4,2,3,1,0:T(8,128)(2,1)S(1)}, u32[]{:S(2)}, u32[]{:S(2)}) async-start(bf16[2,1,16,12,896]{4,2,3,1,0:T(8,128)(2,1)} %copy.74), calls=%async_computation.7 | async-start | bytes 1376256 | tf_op jit(solution)/shard_map/all_to_all | solution.py:68
  394.9 13.7 %all-to-all-start.5 = ((bf16[2,1,16,12,896]{4,2,3,1,0:T(8,128)(2,1)}), bf16[2,1,16,12,896]{4,2,3,1,0:T(8,128)(2,1)S(1)}, u32[]{:S(2)}, u32[]{:S(2)}) async-start(bf16[2,1,16,12,896]{4,2,3,1,0:T(8,128)(2,1)} %copy.65), calls=%async_computation.5 | async-start | bytes 1376256 | tf_op jit(solution)/shard_map/all_to_all | solution.py:68
Sparse Core Ops, SparseCore 0:
  62.6 97.9 all-reduce.6
  261.8 98.9 all-reduce.4
where the time goes:
time: 425 us; the launch traced here: 419 us
  waiting for transfers between devices  217 us (51%)
  matrix products  115 us (27%)
  local copies, waits for them, and re-layouts  35.6 us (8%)
  starting transfers between devices  31.2 us (7%)
  between operations  14.4 us (3%)
  other arithmetic  5.76 us (1%)
    psum x2, waiting for transfers between devices, experts_layer(): summed = lax.psum(rounded.astype(jnp.bfloat16), 'dp').astype(jnp.float32)  196 us
    dot_general x4, matrix products, experts_layer(): jnp.einsum('gmxcd,xdf->gmxcf', arrived, up_weight, preferred_element_type...  57.1 us
    dot_general x4, matrix products, experts_layer(): jnp.einsum('gmxcf,xfd->gmxcd', hidden, down_weight, preferred_element_typ...  56.6 us
    all_to_all x4, starting transfers between devices, experts_layer(): lax.all_to_all(outgoing, 'expert', split_axis=0, concat_axis=0, tiled=True)  14.8 us
    all_to_all x4, starting transfers between devices, experts_layer(): lax.all_to_all(produced, 'expert', split_axis=0, concat_axis=0, tiled=True)  14.3 us
    all_to_all x4, waiting for transfers between devices, experts_layer(): lax.all_to_all(produced, 'expert', split_axis=0, concat_axis=0, tiled=True)  14.2 us
    gather x8, local copies, waits for them, and re-layouts, experts_layer(): flat_tokens[jnp.maximum(source_index, 0)]  9.73 us
  transfers between devices with their start and end apart: 11, of which 6 were waited for; matrix products, arithmetic and copies ran while one was open for 18% of the time, Pallas kernels for 0%

commit v1 on v0

--- a/solution.py
+++ b/solution.py
@@ -60,7 +60,7 @@
         "gmxcd,xdf->gmxcf", arrived, up_weight, preferred_element_type=jnp.float32
     )
     rounded = lax.optimization_barrier(partial_value.astype(jnp.bfloat16)).astype(jnp.float32)
-    summed = lax.psum(rounded.astype(jnp.bfloat16), "dp").astype(jnp.float32)
+    summed = jnp.sum(lax.all_gather(rounded.astype(jnp.bfloat16), "dp"), axis=0).astype(jnp.float32)
     hidden = jax.nn.silu(summed).astype(jnp.bfloat16)
     produced = jnp.einsum(
         "gmxcf,xfd->gmxcd", hidden, down_weight, preferred_element_type=jnp.float32

time: 425 us -> 513 us (1.21)
  blocking collectives: 0 us -> 49 us
  waiting for transfers between devices: 217 us -> 265 us
  starting transfers between devices: 31.2 us -> 15.7 us
  other arithmetic: 5.76 us -> 19 us
    all_gather x0 -> x4, waiting for transfers between devices: none -> 249 us  [experts_layer(): lax.all_gather(rounded.astype(jnp.bfloat16), 'dp')]
    psum x2 -> x0, waiting for transfers between devices: 196 us -> none  [experts_layer(): summed = lax.psum(rounded.astype(jnp.bfloat16), 'dp').astype(jnp.float32)]
    all_to_all x0 -> x4, blocking collectives: none -> 49 us  [experts_layer(): lax.all_to_all(outgoing, 'expert', split_axis=0, concat_axis=0, tiled=True)]
    all_to_all x4 -> x0, starting transfers between devices: 14.8 us -> none  [experts_layer(): lax.all_to_all(outgoing, 'expert', split_axis=0, concat_axis=0, tiled=True)]
    reduce_sum x0 -> x4, other arithmetic: none -> 13.2 us  [experts_layer(): jnp.sum(lax.all_gather(rounded.astype(jnp.bfloat16), 'dp'), axis=0)]
    all_to_all x4 -> x0, waiting for transfers between devices: 6.38 us -> none  [experts_layer(): lax.all_to_all(outgoing, 'expert', split_axis=0, concat_axis=0, tiled=True)]
  transfers between devices with their start and end apart: 11 -> 9, of which waited for: 6 -> 6; matrix products, arithmetic and copies ran while one was open for 18% -> 23% of each run, Pallas kernels for 0% -> 0%
where the time goes in v1:
time: 513 us; the launch traced here: 506 us
  waiting for transfers between devices  265 us (52%)
  matrix products  111 us (22%)
  blocking collectives  49 us (10%)
  local copies, waits for them, and re-layouts  31.8 us (6%)
  other arithmetic  19 us (4%)
  starting transfers between devices  15.7 us (3%)
  between operations  14.1 us (3%)
    all_gather x4, waiting for transfers between devices, experts_layer(): lax.all_gather(rounded.astype(jnp.bfloat16), 'dp')  249 us
    dot_general x4, matrix products, experts_layer(): jnp.einsum('gmxcd,xdf->gmxcf', arrived, up_weight, preferred_element_type...  57.2 us
    dot_general x4, matrix products, experts_layer(): jnp.einsum('gmxcf,xfd->gmxcd', hidden, down_weight, preferred_element_typ...  52.6 us
    all_to_all x4, blocking collectives, experts_layer(): lax.all_to_all(outgoing, 'expert', split_axis=0, concat_axis=0, tiled=True)  49 us
    all_to_all x4, waiting for transfers between devices, experts_layer(): lax.all_to_all(produced, 'expert', split_axis=0, concat_axis=0, tiled=True)  16.1 us
    all_to_all x4, starting transfers between devices, experts_layer(): lax.all_to_all(produced, 'expert', split_axis=0, concat_axis=0, tiled=True)  14.1 us
    reduce_sum x4, other arithmetic, experts_layer(): jnp.sum(lax.all_gather(rounded.astype(jnp.bfloat16), 'dp'), axis=0)  13.2 us
  transfers between devices with their start and end apart: 9, of which 6 were waited for; matrix products, arithmetic and copies ran while one was open for 23% of the time, Pallas kernels for 0%

profile of v1, /device:TPU:0, one launch (start us, length us, event | category | flops | bytes accessed | tf_op | source)
XLA Modules:
  0.0 506.1 jit_solution(11330180440805573082)
XLA Ops:
  8.9 1.4 scatter_custom_fusion.1
  11.3 2.3 gather_fusion.2
  14.2 13.8 %all_to_all.40 = bf16[2,1,16,12,896]{4,2,3,1,0:T(8,128)(2,1)S(1)} all-to-all(bf16[2,1,16,12,896]{4,2,3,1,0:T(8,128)(2,1)S(1)} %copy.54), channel_id=1, replica_groups=mesh['section'=4,'expert'=2,'dp'=4] {'expert'}, dimensions={0} | all-to-all | bytes 1376256 | tf_op jit(solution)/shard_map/all_to_all | solution.py:58
  28.0 14.3 %fusion.34 = bf16[2,1,16,12,1152]{4,3,0,2,1:T(8,128)(2,1)} fusion(bf16[1,16,896,1152]{3,2,1,0:T(8,128)(2,1)} %param.8, bf16[2,1,16,12,896]{4,2,3,1,0:T(8,128)(2,1)S(1)} %all_to_all.40), kind=kOutput, calls=%fused_computation.42 | convolution fusion | flops 793165824 | bytes 34603008 | tf_op jit(solution)/shard_map/gmxcd,xdf->gmxcf/dot_general | solution.py:59
  45.2 2.3 gather_fusion
  48.2 11.7 %all_to_all.41 = bf16[2,1,16,12,896]{4,2,3,1,0:T(8,128)(2,1)S(1)} all-to-all(bf16[2,1,16,12,896]{4,2,3,1,0:T(8,128)(2,1)S(1)} %copy.45), channel_id=1, replica_groups=mesh['section'=4,'expert'=2,'dp'=4] {'expert'}, dimensions={0} | all-to-all | bytes 1376256 | tf_op jit(solution)/shard_map/all_to_all | solution.py:58
  59.8 14.4 %fusion.37 = bf16[2,1,16,12,1152]{4,3,0,2,1:T(8,128)(2,1)} fusion(bf16[1,16,896,1152]{3,2,1,0:T(8,128)(2,1)} %param.8, bf16[2,1,16,12,896]{4,2,3,1,0:T(8,128)(2,1)S(1)} %all_to_all.41), kind=kOutput, calls=%fused_computation.43 | convolution fusion | flops 793165824 | bytes 34603008 | tf_op jit(solution)/shard_map/gmxcd,xdf->gmxcf/dot_general | solution.py:59
  75.9 56.3 %all-gather.11.cloned.1.call-done = bf16[8,1,16,12,1152]{4,3,0,2,1:T(8,128)(2,1)} async-done(((bf16[2,1,16,12,1152]{4,3,0,2,1:T(8,128)(2,1)}), bf16[8,1,16,12,1152]{4,3,0,2,1:T(8,128)(2,1)}) %all-gather.11.cloned.1.call-update) | async-done | bytes 3538960 | tf_op jit(solution)/shard_map/all_gather | solution.py:63
  132.2 3.3 reduce.17
  135.5 13.7 %fusion.74 = bf16[2,1,16,12,896]{4,3,0,2,1:T(8,128)(2,1)S(1)} fusion(bf16[1,16,1152,896]{3,2,1,0:T(8,128)(2,1)} %param.9, bf16[2,16,12,1152]{3,2,0,1:T(8,128)(2,1)S(1)} %reduce.17), kind=kOutput, calls=%fused_computation.66 | convolution fusion | flops 795721728 | bytes 34603008 | tf_op jit(solution)/shard_map/gmxcf,xfd->gmxcd/dot_general | solution.py:65
  150.3 3.5 all-to-all-start.3
  153.9 67.8 %all-gather.9.cloned.1.call-done = bf16[8,1,16,12,1152]{4,3,0,2,1:T(8,128)(2,1)} async-done(((bf16[2,1,16,12,1152]{4,3,0,2,1:T(8,128)(2,1)}), bf16[8,1,16,12,1152]{4,3,0,2,1:T(8,128)(2,1)}) %all-gather.9.cloned.1.call-update) | async-done | bytes 3538960 | tf_op jit(solution)/shard_map/all_gather | solution.py:63
  221.6 3.3 reduce.16
  224.9 12.5 %fusion.77 = bf16[2,1,16,12,896]{4,3,0,2,1:T(8,128)(2,1)S(1)} fusion(bf16[1,16,1152,896]{3,2,1,0:T(8,128)(2,1)} %param.9, bf16[2,16,12,1152]{3,2,0,1:T(8,128)(2,1)S(1)} %reduce.16), kind=kOutput, calls=%fused_computation.67 | convolution fusion | flops 795721728 | bytes 34603008 | tf_op jit(solution)/shard_map/gmxcf,xfd->gmxcd/dot_general | solution.py:65
  238.5 3.5 all-to-all-start.1
  244.1 8.0 %all-to-all-done.1 = bf16[2,1,16,12,896]{4,2,3,1,0:T(8,128)(2,1)S(1)} async-done(((bf16[2,1,16,12,896]{4,2,3,1,0:T(8,128)(2,1)}), bf16[2,1,16,12,896]{4,2,3,1,0:T(8,128)(2,1)S(1)}, u32[]{:S(2)}, u32[]{:S(2)}) %all-to-all-start.1) | async-done | bytes 688160 | tf_op jit(solution)/shard_map/all_to_all | solution.py:68
  254.7 1.5 collective-permute-start
  257.9 2.3 gather_fusion.6
  260.7 11.1 %all_to_all.42 = bf16[2,1,16,12,896]{4,2,3,1,0:T(8,128)(2,1)S(1)} all-to-all(bf16[2,1,16,12,896]{4,2,3,1,0:T(8,128)(2,1)S(1)} %copy.72), channel_id=1, replica_groups=mesh['section'=4,'expert'=2,'dp'=4] {'expert'}, dimensions={0} | all-to-all | bytes 1376256 | tf_op jit(solution)/shard_map/all_to_all | solution.py:58
  271.8 14.3 %fusion.28 = bf16[2,1,16,12,1152]{4,3,0,2,1:T(8,128)(2,1)} fusion(bf16[1,16,896,1152]{3,2,1,0:T(8,128)(2,1)} %param.8, bf16[2,1,16,12,896]{4,2,3,1,0:T(8,128)(2,1)S(1)} %all_to_all.42), kind=kOutput, calls=%fused_computation.40 | convolution fusion | flops 793165824 | bytes 34603008 | tf_op jit(solution)/shard_map/gmxcd,xdf->gmxcf/dot_general | solution.py:59
  289.2 2.3 gather_fusion.4
  292.0 12.4 %all_to_all.43 = bf16[2,1,16,12,896]{4,2,3,1,0:T(8,128)(2,1)S(1)} all-to-all(bf16[2,1,16,12,896]{4,2,3,1,0:T(8,128)(2,1)S(1)} %copy.63), channel_id=1, replica_groups=mesh['section'=4,'expert'=2,'dp'=4] {'expert'}, dimensions={0} | all-to-all | bytes 1376256 | tf_op jit(solution)/shard_map/all_to_all | solution.py:58
  304.4 14.3 %fusion.31 = bf16[2,1,16,12,1152]{4,3,0,2,1:T(8,128)(2,1)} fusion(bf16[1,16,896,1152]{3,2,1,0:T(8,128)(2,1)} %param.8, bf16[2,1,16,12,896]{4,2,3,1,0:T(8,128)(2,1)S(1)} %all_to_all.43), kind=kOutput, calls=%fused_computation.41 | convolution fusion | flops 793165824 | bytes 34603008 | tf_op jit(solution)/shard_map/gmxcd,xdf->gmxcf/dot_general | solution.py:59
  318.9 57.3 %all-gather.15.cloned.1.call-done = bf16[8,1,16,12,1152]{4,3,0,2,1:T(8,128)(2,1)} async-done(((bf16[2,1,16,12,1152]{4,3,0,2,1:T(8,128)(2,1)}), bf16[8,1,16,12,1152]{4,3,0,2,1:T(8,128)(2,1)}) %all-gather.15.cloned.1.call-update) | async-done | bytes 3538960 | tf_op jit(solution)/shard_map/all_gather | solution.py:63
  376.2 3.3 reduce.19
  379.5 13.7 %fusion.68 = bf16[2,1,16,12,896]{4,3,0,2,1:T(8,128)(2,1)S(1)} fusion(bf16[1,16,1152,896]{3,2,1,0:T(8,128)(2,1)} %param.9, bf16[2,16,12,1152]{3,2,0,1:T(8,128)(2,1)S(1)} %reduce.19), kind=kOutput, calls=%fused_computation.64 | convolution fusion | flops 795721728 | bytes 34603008 | tf_op jit(solution)/shard_map/gmxcf,xfd->gmxcd/dot_general | solution.py:65
  394.3 3.5 all-to-all-start.7
  397.8 67.6 %all-gather.13.cloned.1.call-done = bf16[8,1,16,12,1152]{4,3,0,2,1:T(8,128)(2,1)} async-done(((bf16[2,1,16,12,1152]{4,3,0,2,1:T(8,128)(2,1)}), bf16[8,1,16,12,1152]{4,3,0,2,1:T(8,128)(2,1)}) %all-gather.13.cloned.1.call-update) | async-done | bytes 3538960 | tf_op jit(solution)/shard_map/all_gather | solution.py:63
  465.5 3.3 reduce.18
  468.8 12.5 %fusion.71 = bf16[2,1,16,12,896]{4,3,0,2,1:T(8,128)(2,1)S(1)} fusion(bf16[1,16,1152,896]{3,2,1,0:T(8,128)(2,1)} %param.9, bf16[2,16,12,1152]{3,2,0,1:T(8,128)(2,1)S(1)} %reduce.18), kind=kOutput, calls=%fused_computation.65 | convolution fusion | flops 795721728 | bytes 34603008 | tf_op jit(solution)/shard_map/gmxcf,xfd->gmxcd/dot_general | solution.py:65
  482.4 3.5 all-to-all-start.5
  487.9 8.1 %all-to-all-done.5 = bf16[2,1,16,12,896]{4,2,3,1,0:T(8,128)(2,1)S(1)} async-done(((bf16[2,1,16,12,896]{4,2,3,1,0:T(8,128)(2,1)}), bf16[2,1,16,12,896]{4,2,3,1,0:T(8,128)(2,1)S(1)}, u32[]{:S(2)}, u32[]{:S(2)}) %all-to-all-start.5) | async-done | bytes 688160 | tf_op jit(solution)/shard_map/all_to_all | solution.py:68
  (157 shorter events, 28.9 us)
Async XLA Ops:
  6.5 125.7 %all-gather.11.cloned.1.call-start = ((), (), s32[]{:S(2)}) async-start(), calls=%async_computation.9 | async-start | bytes 5898240 | tf_op jit(solution)/shard_map/all_gather | solution.py:63
  42.3 179.4 %all-gather.9.cloned.1.call-start = ((), (), s32[]{:S(2)}) async-start(), calls=%async_computation.8 | async-start | bytes 5898240 | tf_op jit(solution)/shard_map/all_gather | solution.py:63
  59.8 15.9 %copy-start.2 = (f32[2,1,2,64,4]{3,4,2,1,0:T(4,128)S(1)}, f32[2,1,2,64,4]{3,4,2,1,0:T(4,128)}, u32[]{:S(2)}) copy-start(f32[2,1,2,64,4]{3,4,2,1,0:T(4,128)} %param.11) | copy-start | bytes 12292
  150.3 88.2 %all-to-all-start.3 = ((bf16[2,1,16,12,896]{4,2,3,1,0:T(8,128)(2,1)}), bf16[2,1,16,12,896]{4,2,3,1,0:T(8,128)(2,1)S(1)}, u32[]{:S(2)}, u32[]{:S(2)}) async-start(bf16[2,1,16,12,896]{4,2,3,1,0:T(8,128)(2,1)} %copy.56), calls=%async_computation.3 | async-start | bytes 1376256 | tf_op jit(solution)/shard_map/all_to_all | solution.py:68
  238.5 13.6 %all-to-all-start.1 = ((bf16[2,1,16,12,896]{4,2,3,1,0:T(8,128)(2,1)}), bf16[2,1,16,12,896]{4,2,3,1,0:T(8,128)(2,1)S(1)}, u32[]{:S(2)}, u32[]{:S(2)}) async-start(bf16[2,1,16,12,896]{4,2,3,1,0:T(8,128)(2,1)} %copy.47), calls=%async_computation.1 | async-start | bytes 1376256 | tf_op jit(solution)/shard_map/all_to_all | solution.py:68
  242.1 134.1 %all-gather.15.cloned.1.call-start = ((), (), s32[]{:S(2)}) async-start(), calls=%async_computation.11 | async-start | bytes 5898240 | tf_op jit(solution)/shard_map/all_gather | solution.py:63
  253.7 1.0 copy-start
  253.7 4.2 copy-start.1
  254.7 3.1 collective-permute-start
  286.1 179.4 %all-gather.13.cloned.1.call-start = ((), (), s32[]{:S(2)}) async-start(), calls=%async_computation.10 | async-start | bytes 5898240 | tf_op jit(solution)/shard_map/all_gather | solution.py:63
  394.3 88.1 %all-to-all-start.7 = ((bf16[2,1,16,12,896]{4,2,3,1,0:T(8,128)(2,1)}), bf16[2,1,16,12,896]{4,2,3,1,0:T(8,128)(2,1)S(1)}, u32[]{:S(2)}, u32[]{:S(2)}) async-start(bf16[2,1,16,12,896]{4,2,3,1,0:T(8,128)(2,1)} %copy.74), calls=%async_computation.7 | async-start | bytes 1376256 | tf_op jit(solution)/shard_map/all_to_all | solution.py:68
  482.4 13.6 %all-to-all-start.5 = ((bf16[2,1,16,12,896]{4,2,3,1,0:T(8,128)(2,1)}), bf16[2,1,16,12,896]{4,2,3,1,0:T(8,128)(2,1)S(1)}, u32[]{:S(2)}, u32[]{:S(2)}) async-start(bf16[2,1,16,12,896]{4,2,3,1,0:T(8,128)(2,1)} %copy.65), calls=%async_computation.5 | async-start | bytes 1376256 | tf_op jit(solution)/shard_map/all_to_all | solution.py:68
Sparse Core Ops, SparseCore 0:
  42.4 89.7 all-gather.10
  133.8 87.8 all-gather.8
  286.2 89.9 all-gather.14
  377.6 87.8 all-gather.12
